TPU v7x, 256 devices: a whole 4x4x8 slice. The times are simulated.
256 devices in a mesh: seq: 32 (over z, x), exp: 8 (over y, core).
Axes of the slice: x: 4, y: 4, z: 8, core: 2. Of those that a mesh axis runs over, the one named last changes fastest.
Arguments:
- x_resid: bfloat16 [16384, 2048], P(('seq', 'exp')), may hold values from -36 to 36
- queries: bfloat16 [16384, 2048], P('seq', 'exp'), may hold values from -6 to 6
- key_proj: bfloat16 [16384, 2048], P('seq', 'exp'), may hold values from -6 to 6
- val_proj: bfloat16 [16384, 2048], P('seq', 'exp'), may hold values from -6 to 6
- w_out: bfloat16 [2048, 2048], P('exp'), may hold values from -0.125 to 0.125
- norm_gain: float32 [2048], replicated, may hold values from 0.1 to 1.9
- w_gate: bfloat16 [8, 2048, 1408], P('exp', 'seq'), may hold values from -0.125 to 0.125
- w_up: bfloat16 [8, 2048, 1408], P('exp', 'seq'), may hold values from -0.125 to 0.125
- w_down: bfloat16 [8, 1408, 2048], P('exp', None, 'seq'), may hold values from -0.15625 to 0.15625
- routes: int32 [16384, 2], P(('seq', 'exp')), may hold values from 0 to 7, all different within a row; in each aligned block of 64 rows (0 to 63, 64 to 127, ...) at most 18 rows name the same one
- gate_prob: float32 [16384, 2], P(('seq', 'exp')), may hold values from 0.05 to 0.6
- grad_out: bfloat16 [16384, 2048], P(('seq', 'exp')), may hold values from -6 to 6
Outputs:
- layer_out: bfloat16 [16384, 2048], P(('seq', 'exp'))
- grad_in: bfloat16 [16384, 2048], P(('seq', 'exp'))
- grad_gate: float32 [16384, 2], P(('seq', 'exp'))
Inputs may be any that keep to these rules, and one draw needn't show every extreme that they name: `routes`: in each aligned block of 64 tokens (the tokens of one device) no expert is named by more than 18 rows, a bound that some block reaches; a token's two experts differ.
All inputs are finite; a program needn't handle non-finite values.
Results may differ from a plain program's by a relative error of at most 0.024.
Values may be sent and summed in bfloat16 or wider, within the bound.
No kernel may reach another device: no remote copies, remote signals or barrier semaphores. Data moves between devices by JAX's collectives and lax.ppermute only.
A program may use at most 128 MiB of HBM per device.

v0:
```python
import math

import jax
import jax.numpy as jnp
from jax import lax
from jax.sharding import PartitionSpec as P

HD = 128
W = 2048


norm_eps = 1e-06


def from_behind(block, axis, distance):
    devices = range(lax.axis_size(axis))
    route = [(i - distance, i) for i in devices if i - distance in devices]
    return lax.ppermute(block, axis, route)


def window_attention(queries, key_rows, val_rows, seq_base):
    tok_seq = queries.shape[0]
    feat_width = queries.shape[1]
    head_count = feat_width // HD
    key_span = key_rows.shape[0]
    reach_len = key_span - tok_seq
    block_rows = min(512, tok_seq)
    key_heads = key_rows.reshape(key_span, head_count, HD)
    val_heads = val_rows.reshape(key_span, head_count, HD)
    score_scale = 1.0 / math.sqrt(HD)
    key_pos = seq_base - reach_len + jnp.arange(key_span, dtype=jnp.int32)
    query_heads = queries.reshape(block_rows, head_count, HD)
    scores = (
        jnp.einsum("qhd,khd->hqk", query_heads, key_heads, preferred_element_type=jnp.float32)
        * score_scale
    )
    query_pos = seq_base + 0 + jnp.arange(block_rows, dtype=jnp.int32)
    offset = query_pos[:, None] - key_pos[None, :]
    allowed = (offset >= 0) & (offset < reach_len) & (key_pos[None, :] >= 0)
    scores = jnp.where(allowed[None], scores, -jnp.inf)
    row_max = jnp.max(scores, axis=-1, keepdims=True)
    exp_scores = jnp.exp(scores - row_max)
    weights = (exp_scores / jnp.sum(exp_scores, axis=-1, keepdims=True)).astype(jnp.bfloat16)
    mixed_rows = jnp.einsum("hqk,khd->qhd", weights, val_heads, preferred_element_type=jnp.float32)
    pieces = mixed_rows.reshape(block_rows, feat_width).astype(jnp.bfloat16)
    return pieces


def per_device(
    x_resid,
    queries,
    key_proj,
    val_proj,
    w_out,
    norm_gain,
    w_gate,
    w_up,
    w_down,
    routes,
    gate_prob,
    grad_out,
):
    tok_seq = queries.shape[0]
    hop_count = W // tok_seq
    seq_base = lax.axis_index("seq") * tok_seq
    earlier = []
    carried = (key_proj, val_proj)
    for hop_index in range(hop_count):
        carried = from_behind((carried[0], carried[1]), "seq", 1)
        earlier.insert(0, carried)
    key_rows = jnp.concatenate([pair[0] for pair in earlier] + [key_proj], axis=0)
    val_rows = jnp.concatenate([pair[1] for pair in earlier] + [val_proj], axis=0)
    attn = window_attention(queries, key_rows, val_rows, seq_base)
    tok_dev = x_resid.shape[0]
    model_width = x_resid.shape[1]
    projected = lax.psum_scatter(
        jnp.dot(attn, w_out, preferred_element_type=jnp.float32).astype(jnp.bfloat16),
        "exp",
        scatter_dimension=0,
        tiled=True,
    ).astype(jnp.float32)
    hidden_state = (x_resid.astype(jnp.float32) + projected).astype(jnp.bfloat16)
    hidden_f = hidden_state.astype(jnp.float32)
    rstd_rows = lax.rsqrt(jnp.mean(hidden_f * hidden_f, axis=-1, keepdims=True) + norm_eps)
    normed = hidden_f * rstd_rows
    moe_in = (normed * norm_gain).astype(jnp.bfloat16)
    exp_size = lax.axis_size("exp")
    local_experts = w_gate.shape[0]
    expert_count = local_experts * exp_size
    capacity = 9 * tok_dev // (4 * expert_count)
    flat_routes = routes.reshape(-1)
    row_total = flat_routes.shape[0]
    one_hot = (flat_routes[:, None] == jnp.arange(expert_count, dtype=jnp.int32)[None, :]).astype(
        jnp.int32
    )
    before = jnp.cumsum(one_hot, axis=0) - one_hot
    slot_rank = jnp.sum(before * one_hot, axis=1)
    target = flat_routes * capacity + slot_rank
    slot_source = (
        jnp.full((expert_count * capacity,), row_total, jnp.int32)
        .at[target]
        .set(jnp.arange(row_total, dtype=jnp.int32))
    )
    token_of_slot = slot_source // 2
    padded_in = jnp.concatenate([moe_in, jnp.zeros((1, model_width), jnp.bfloat16)], axis=0)
    padded_grad = jnp.concatenate([grad_out, jnp.zeros((1, model_width), jnp.bfloat16)], axis=0)
    send_in = jnp.take(padded_in, token_of_slot, axis=0).reshape(
        expert_count, capacity, model_width
    )
    send_grad = jnp.take(padded_grad, token_of_slot, axis=0).reshape(
        expert_count, capacity, model_width
    )
    gate_full, up_full, down_full = (
        lax.all_gather(w_gate, "seq", axis=1, tiled=True),
        lax.all_gather(w_up, "seq", axis=1, tiled=True),
        lax.all_gather(w_down, "seq", axis=2, tiled=True),
    )
    recv_in = lax.all_to_all(send_in, "exp", split_axis=0, concat_axis=0, tiled=True)
    recv_grad = lax.all_to_all(send_grad, "exp", split_axis=0, concat_axis=0, tiled=True)
    slot_count = recv_in.shape[1]
    shaped_in = recv_in.reshape(exp_size, local_experts, slot_count, model_width)
    shaped_grad = recv_grad.reshape(exp_size, local_experts, slot_count, model_width)
    gate_pre = jnp.einsum(
        "necd,edh->nech", shaped_in, gate_full, preferred_element_type=jnp.float32
    )
    up_pre = jnp.einsum("necd,edh->nech", shaped_in, up_full, preferred_element_type=jnp.float32)
    sigma = jax.nn.sigmoid(gate_pre)
    act_vals = gate_pre * sigma
    expert_hidden = (act_vals * up_pre).astype(jnp.bfloat16)
    expert_out = jnp.einsum(
        "nech,ehd->necd", expert_hidden, down_full, preferred_element_type=jnp.float32
    ).astype(jnp.bfloat16)
    back_hidden = jnp.einsum(
        "necd,ehd->nech", shaped_grad, down_full, preferred_element_type=jnp.float32
    )
    grad_pre_gate = (back_hidden * up_pre * sigma * (1.0 + gate_pre * (1.0 - sigma))).astype(
        jnp.bfloat16
    )
    grad_pre_up = (back_hidden * act_vals).astype(jnp.bfloat16)
    row_grad = jnp.einsum(
        "nech,edh->necd", grad_pre_gate, gate_full, preferred_element_type=jnp.float32
    )
    row_grad = row_grad + jnp.einsum(
        "nech,edh->necd", grad_pre_up, up_full, preferred_element_type=jnp.float32
    )
    flat_out = expert_out.reshape(exp_size * local_experts, slot_count, model_width)
    flat_back = row_grad.astype(jnp.bfloat16).reshape(
        exp_size * local_experts, slot_count, model_width
    )
    back_out = lax.all_to_all(flat_out, "exp", split_axis=0, concat_axis=0, tiled=True)
    back_grad = lax.all_to_all(flat_back, "exp", split_axis=0, concat_axis=0, tiled=True)
    row_out = jnp.take(back_out.reshape(expert_count * capacity, model_width), target, axis=0)
    row_out = row_out.reshape(tok_dev, 2, model_width).astype(jnp.float32)
    row_back = jnp.take(back_grad.reshape(expert_count * capacity, model_width), target, axis=0)
    row_back = row_back.reshape(tok_dev, 2, model_width).astype(jnp.float32)
    layer_out = (hidden_f + jnp.sum(gate_prob[:, :, None] * row_out, axis=1)).astype(jnp.bfloat16)
    grad_float = grad_out.astype(jnp.float32)
    grad_gate = jnp.sum(grad_float[:, None, :] * row_out, axis=2)
    moe_grad = jnp.sum(gate_prob[:, :, None] * row_back, axis=1)
    scaled = moe_grad * norm_gain
    grad_in = grad_float + rstd_rows * (
        scaled - normed * jnp.mean(scaled * normed, axis=-1, keepdims=True)
    )
    return (layer_out, grad_in.astype(jnp.bfloat16), grad_gate)


def solution(mesh):
    placed = (
        P(("seq", "exp"), None),
        P("seq", "exp"),
        P("seq", "exp"),
        P("seq", "exp"),
        P("exp", None),
        P(),
        P("exp", "seq", None),
        P("exp", "seq", None),
        P("exp", None, "seq"),
        P(("seq", "exp"), None),
        P(("seq", "exp"), None),
        P(("seq", "exp"), None),
    )
    return jax.shard_map(
        per_device,
        mesh=mesh,
        in_specs=placed,
        out_specs=(P(("seq", "exp"), None), P(("seq", "exp"), None), P(("seq", "exp"), None)),
        check_vma=False,
    )
```

profile of v0, /device:TPU:2, one launch (start us, length us, event | category | flops | bytes accessed | tf_op | source)
XLA Modules:
  0.0 416.7 jit_solution(17349679313935486724)
XLA Ops:
  8.1 3.5 collective-permute-start
  11.6 1.1 copy.35
  12.7 3.1 collective-permute-start.4
  15.8 3.7 collective-permute-done
  19.5 3.4 collective-permute-start.1
  22.9 2.2 collective-permute-done.4
  25.1 3.4 collective-permute-start.5
  28.5 2.2 collective-permute-done.1
  30.7 3.4 collective-permute-start.2
  34.2 2.2 collective-permute-done.5
  36.3 3.4 collective-permute-start.6
  39.7 2.2 collective-permute-done.2
  42.0 3.4 collective-permute-start.3
  45.4 3.0 fusion.17
  48.4 4.3 %collective-permute-start.7 = (bf16[512,256]{0,1:T(8,128)(2,1)}, bf16[512,256]{0,1:T(8,128)(2,1)}, u32[]{:S(2)}, u32[]{:S(2)}) collective-permute-start(bf16[512,256]{0,1:T(8,128)(2,1)} %collective-permute-done.6), channel_id=1, source_target_pairs={{0,8},{8,16},{16,24},{24,32},{32,40},{40,48},{48,56},{56,64},{64,7... | collective-permute-start | bytes 786440 | tf_op jit(solution)/shard_map/ppermute | solution.py:18
  54.3 1.6 copy.34
  55.9 1.8 collective-permute-done.7
  59.8 5.6 %fusion.60 = f32[2,2560,512]{2,1,0:T(8,128)} fusion(bf16[2560,2,128]{0,2,1:T(8,128)(2,1)S(1)} %bitcast.105, bf16[512,256]{1,0:T(8,128)(2,1)S(1)} %copy-done.7), kind=kOutput, calls=%fused_computation.70 | convolution fusion | flops 671088640 | bytes 12058624 | tf_op jit(solution)/shard_map/qhd,khd->hqk/dot_general | solution.py:34
  65.4 5.1 %fusion.80 = f32[2,512]{1,0:T(2,128)S(1)} fusion(pred[512,2560]{0,1:T(8,128)(4,1)} %fusion.17, bf16[2560,2,128]{0,2,1:T(8,128)(2,1)S(1)} %bitcast.106, bf16[512,256]{1,0:T(8,128)(2,1)S(1)} %copy-done.7), kind=kOutput, calls=%fused_computation.115 | convolution fusion | flops 681576960 | bytes 2887680 | tf_op jit(solution)/shard_map/sub | solution.py:42
  70.4 8.7 %fusion.38 = bf16[2,128,512]{2,1,0:T(8,128)(2,1)S(1)} fusion(bf16[2560,2,128]{0,2,1:T(8,128)(2,1)} %bitcast.107, f32[2,512]{1,0:T(2,128)S(1)} %fusion.80, f32[2,2560,512]{2,1,0:T(8,128)} %fusion.60, pred[512,2560]{0,1:T(8,128)(4,1)} %fusion.17), kind=kOutput, calls=%fused_computation.37 | convolution fusion | flops 684330496 | bytes 13373440 | tf_op jit(solution)/shard_map/hqk,khd->qhd/dot_general | solution.py:44
  79.1 2.1 convolution_convert_fusion
  84.0 1.2 scatter_custom_fusion
  86.2 41.6 %reduce-scatter.2.cloned.1.call-done = bf16[64,2048]{1,0:T(8,128)(2,1)} async-done(((bf16[512,2048]{1,0:T(8,128)(2,1)}), bf16[64,2048]{1,0:T(8,128)(2,1)}) %reduce-scatter.2.cloned.1.call-update) | async-done | bytes 262160 | tf_op jit(solution)/shard_map/reduce_scatter | solution.py:76
  127.8 1.1 fusion.54
  131.2 2.1 reshape.194
  133.3 3.5 all-to-all-start
  136.8 1.0 reshape.200
  137.9 12.0 %all-to-all-done = bf16[8,18,2048]{2,1,0:T(8,128)(2,1)S(1)} async-done(((bf16[8,18,2048]{2,1,0:T(8,128)(2,1)}), bf16[8,18,2048]{2,1,0:T(8,128)(2,1)S(1)}, u32[]{:S(2)}, u32[]{:S(2)}) %all-to-all-start) | async-done | bytes 589856 | tf_op jit(solution)/shard_map/all_to_all | solution.py:118
  150.8 3.6 all-to-all-start.2
  154.4 25.0 %all-gather.6.cloned.1.call-done = bf16[1,2048,1408]{2,1,0:T(8,128)(2,1)} async-done(((bf16[1,64,1408]{2,1,0:T(8,128)(2,1)}), bf16[1,2048,1408]{2,1,0:T(8,128)(2,1)}) %all-gather.6.cloned.1.call-update) | async-done | bytes 5767184 | tf_op jit(solution)/shard_map/all_gather | solution.py:115
  179.4 5.3 %fusion.23 = f32[8,1,18,1408]{3,2,0,1:T(8,128)} fusion(bf16[8,18,2048]{2,1,0:T(8,128)(2,1)} %copy-done.5, bf16[1,2048,1408]{2,1,0:T(8,128)(2,1)} %all-gather.6.cloned.1.call-done), kind=kOutput, calls=%fused_computation.32 | convolution fusion | flops 830472192 | bytes 7168000 | tf_op jit(solution)/shard_map/necd,edh->nech/dot_general | solution.py:126
  184.7 80.9 %all-gather.4.cloned.1.call-done = bf16[1,2048,1408]{2,1,0:T(8,128)(2,1)} async-done(((bf16[1,64,1408]{2,1,0:T(8,128)(2,1)}), bf16[1,2048,1408]{2,1,0:T(8,128)(2,1)}) %all-gather.4.cloned.1.call-update) | async-done | bytes 5767184 | tf_op jit(solution)/shard_map/all_gather | solution.py:114
  265.6 5.0 %fusion.20 = f32[8,1,18,1408]{3,2,0,1:T(8,128)} fusion(bf16[8,18,2048]{2,1,0:T(8,128)(2,1)S(1)} %copy-done.6, bf16[1,2048,1408]{2,1,0:T(8,128)(2,1)} %all-gather.4.cloned.1.call-done), kind=kOutput, calls=%fused_computation.31 | convolution fusion | flops 830472192 | bytes 7168000 | tf_op jit(solution)/shard_map/necd,edh->nech/dot_general | solution.py:123
  270.6 81.2 %all-gather.8.cloned.1.call-done = bf16[1,1408,2048]{1,2,0:T(8,128)(2,1)} async-done(((bf16[1,1408,64]{1,2,0:T(8,128)(2,1)}), bf16[1,1408,2048]{1,2,0:T(8,128)(2,1)}) %all-gather.8.cloned.1.call-update) | async-done | bytes 5767184 | tf_op jit(solution)/shard_map/all_gather | solution.py:116
  351.8 6.4 %fusion.35 = bf16[8,18,2048]{2,1,0:T(8,128)(2,1)} fusion(bf16[1,1408,2048]{1,2,0:T(8,128)(2,1)} %all-gather.8.cloned.1.call-done, f32[8,1,18,1408]{3,2,0,1:T(8,128)} %fusion.23, f32[8,1,18,1408]{3,2,0,1:T(8,128)} %fusion.20), kind=kOutput, calls=%fused_computation.36 | convolution fusion | flops 831983616 | bytes 7979008 | tf_op jit(solution)/shard_map/nech,ehd->necd/dot_general | solution.py:130
  358.2 4.3 %all-to-all-start.1 = ((bf16[8,18,2048]{2,1,0:T(8,128)(2,1)}), bf16[8,18,2048]{2,1,0:T(8,128)(2,1)S(1)}, u32[]{:S(2)}, u32[]{:S(2)}) async-start(bf16[8,18,2048]{2,1,0:T(8,128)(2,1)} %fusion.35), calls=%async_computation.2 | async-start | bytes 1572864 | tf_op jit(solution)/shard_map/all_to_all | solution.py:150
  362.5 4.2 %fusion.26 = f32[8,1,18,1408]{3,2,0,1:T(8,128)S(1)} fusion(bf16[8,18,2048]{2,1,0:T(8,128)(2,1)S(1)} %all-to-all-done.2, bf16[1,1408,2048]{1,2,0:T(8,128)(2,1)} %all-gather.8.cloned.1.call-done), kind=kOutput, calls=%fused_computation.33 | convolution fusion | flops 830472192 | bytes 7168000 | tf_op jit(solution)/shard_map/necd,ehd->nech/dot_general | solution.py:133
  366.7 5.0 %fusion.6 = f32[8,18,2048]{2,1,0:T(8,128)S(1)} fusion(bf16[1,2048,1408]{2,1,0:T(8,128)(2,1)} %all-gather.6.cloned.1.call-done, f32[8,1,18,1408]{3,2,0,1:T(8,128)S(1)} %fusion.26, f32[8,1,18,1408]{3,2,0,1:T(8,128)S(1)} %copy-done.17), kind=kOutput, calls=%fused_computation.16 | convolution fusion | flops 831688704 | bytes 8568832 | tf_op jit(solution)/shard_map/nech,edh->necd/dot_general | solution.py:143
  371.8 3.2 fusion.32
  375.7 4.4 %all-to-all-start.3 = ((bf16[8,18,2048]{2,1,0:T(8,128)(2,1)}), bf16[8,18,2048]{2,1,0:T(8,128)(2,1)}, u32[]{:S(2)}, u32[]{:S(2)}) async-start(bf16[8,18,2048]{2,1,0:T(8,128)(2,1)} %fusion.32), calls=%async_computation.4 | async-start | bytes 1572864 | tf_op jit(solution)/shard_map/all_to_all | solution.py:151
  380.2 1.5 mul.153
  381.7 1.7 mul.154
  384.5 8.6 %all-to-all-done.3 = bf16[8,18,2048]{2,1,0:T(8,128)(2,1)} async-done(((bf16[8,18,2048]{2,1,0:T(8,128)(2,1)}), bf16[8,18,2048]{2,1,0:T(8,128)(2,1)}, u32[]{:S(2)}, u32[]{:S(2)}) %all-to-all-start.3) | async-done | bytes 589856 | tf_op jit(solution)/shard_map/all_to_all | solution.py:151
  393.1 1.3 reshape.203
  395.4 1.5 select_convert_fusion.1
  396.9 1.8 reshape.205
  398.7 2.8 reshape.204
  401.6 5.2 %multiply_reduce_fusion.1 = (f32[64,2048]{1,0:T(8,128)S(1)}, f32[64,2048]{1,0:T(8,128)}) fusion(f32[64,2,2048]{2,1,0:T(2,128)S(1)} %reshape.205, f32[64,2]{1,0:T(8,128)S(1)} %copy.40, f32[64,2,2048]{2,1,0:T(2,128)} %reshape.204), kind=kLoop, calls=%fused_computation.44 | loop fusion | flops 786432 | bytes 3146240 | tf_op jit(solution)/shard_map/reduce_sum | solution.py:159
  (97 shorter events, 15.5 us)
Async XLA Ops:
  8.0 71.1 %copy-start = (bf16[256,2048]{1,0:T(8,128)(2,1)S(1)}, bf16[256,2048]{1,0:T(8,128)(2,1)}, u32[]{:S(2)}) copy-start(bf16[256,2048]{1,0:T(8,128)(2,1)} %param.20) | copy-start | bytes 3145732
  8.0 119.8 %reduce-scatter.2.cloned.1.call-start = ((), (), s32[]{:S(2)}) async-start(), calls=%async_computation.5 | async-start | bytes 2359296 | tf_op jit(solution)/shard_map/reduce_scatter | solution.py:76
  8.1 11.4 %collective-permute-start = (bf16[512,256]{1,0:T(8,128)(2,1)}, bf16[512,256]{1,0:T(8,128)(2,1)S(1)}, u32[]{:S(2)}, u32[]{:S(2)}) collective-permute-start(bf16[512,256]{1,0:T(8,128)(2,1)} %param.19), channel_id=1, source_target_pairs={{0,8},{8,16},{16,24},{24,32},{32,40},{40,48},{48,56},{56,64},{64,7... | collective-permute-start | bytes 786440 | tf_op jit(solution)/shard_map/ppermute | solution.py:18
  12.7 12.4 %collective-permute-start.4 = (bf16[512,256]{0,1:T(8,128)(2,1)S(1)}, bf16[512,256]{0,1:T(8,128)(2,1)S(1)}, u32[]{:S(2)}, u32[]{:S(2)}) collective-permute-start(bf16[512,256]{0,1:T(8,128)(2,1)S(1)} %copy.35), channel_id=1, source_target_pairs={{0,8},{8,16},{16,24},{24,32},{32,40},{40,48},{48,56},{56,64},{64,7... | collective-permute-start | bytes 786440 | tf_op jit(solution)/shard_map/ppermute | solution.py:18
  19.5 11.2 %collective-permute-start.1 = (bf16[512,256]{1,0:T(8,128)(2,1)S(1)}, bf16[512,256]{1,0:T(8,128)(2,1)S(1)}, u32[]{:S(2)}, u32[]{:S(2)}) collective-permute-start(bf16[512,256]{1,0:T(8,128)(2,1)S(1)} %collective-permute-done), channel_id=1, source_target_pairs={{0,8},{8,16},{16,24},{24,32},{32,40},{40,48},{48,56},{56,64},{64,7... | collective-permute-start | bytes 786440 | tf_op jit(solution)/shard_map/ppermute | solution.py:18
  25.1 11.2 %collective-permute-start.5 = (bf16[512,256]{0,1:T(8,128)(2,1)S(1)}, bf16[512,256]{0,1:T(8,128)(2,1)S(1)}, u32[]{:S(2)}, u32[]{:S(2)}) collective-permute-start(bf16[512,256]{0,1:T(8,128)(2,1)S(1)} %collective-permute-done.4), channel_id=1, source_target_pairs={{0,8},{8,16},{16,24},{24,32},{32,40},{40,48},{48,56},{56,64},{64,7... | collective-permute-start | bytes 786440 | tf_op jit(solution)/shard_map/ppermute | solution.py:18
  30.7 11.2 %collective-permute-start.2 = (bf16[512,256]{1,0:T(8,128)(2,1)S(1)}, bf16[512,256]{1,0:T(8,128)(2,1)S(1)}, u32[]{:S(2)}, u32[]{:S(2)}) collective-permute-start(bf16[512,256]{1,0:T(8,128)(2,1)S(1)} %collective-permute-done.1), channel_id=1, source_target_pairs={{0,8},{8,16},{16,24},{24,32},{32,40},{40,48},{48,56},{56,64},{64,7... | collective-permute-start | bytes 786440 | tf_op jit(solution)/shard_map/ppermute | solution.py:18
  36.3 16.4 %copy-start.9 = (bf16[512,256]{0,1:T(8,128)(2,1)}, bf16[512,256]{0,1:T(8,128)(2,1)S(1)}, u32[]{:S(2)}) copy-start(bf16[512,256]{0,1:T(8,128)(2,1)S(1)} %collective-permute-done.5) | copy-start | bytes 786436
  36.3 12.1 %collective-permute-start.6 = (bf16[512,256]{0,1:T(8,128)(2,1)S(1)}, bf16[512,256]{0,1:T(8,128)(2,1)}, u32[]{:S(2)}, u32[]{:S(2)}) collective-permute-start(bf16[512,256]{0,1:T(8,128)(2,1)S(1)} %collective-permute-done.5), channel_id=1, source_target_pairs={{0,8},{8,16},{16,24},{24,32},{32,40},{40,48},{48,56},{56,64},{64,7... | collective-permute-start | bytes 786440 | tf_op jit(solution)/shard_map/ppermute | solution.py:18
  42.0 10.8 %copy-start.11 = (bf16[512,256]{1,0:T(8,128)(2,1)}, bf16[512,256]{1,0:T(8,128)(2,1)S(1)}, u32[]{:S(2)}) copy-start(bf16[512,256]{1,0:T(8,128)(2,1)S(1)} %collective-permute-done.2) | copy-start | bytes 786436
  42.0 11.2 %collective-permute-start.3 = (bf16[512,256]{1,0:T(8,128)(2,1)S(1)}, bf16[512,256]{1,0:T(8,128)(2,1)S(1)}, u32[]{:S(2)}, u32[]{:S(2)}) collective-permute-start(bf16[512,256]{1,0:T(8,128)(2,1)S(1)} %collective-permute-done.2), channel_id=1, source_target_pairs={{0,8},{8,16},{16,24},{24,32},{32,40},{40,48},{48,56},{56,64},{64,7... | collective-permute-start | bytes 786440 | tf_op jit(solution)/shard_map/ppermute | solution.py:18
  48.4 5.9 %copy-start.8 = (bf16[512,256]{1,0:T(8,128)(2,1)S(1)}, bf16[512,256]{1,0:T(8,128)(2,1)}, u32[]{:S(2)}) copy-start(bf16[512,256]{1,0:T(8,128)(2,1)} %param.19) | copy-start | bytes 786436
  48.4 9.4 %collective-permute-start.7 = (bf16[512,256]{0,1:T(8,128)(2,1)}, bf16[512,256]{0,1:T(8,128)(2,1)}, u32[]{:S(2)}, u32[]{:S(2)}) collective-permute-start(bf16[512,256]{0,1:T(8,128)(2,1)} %collective-permute-done.6), channel_id=1, source_target_pairs={{0,8},{8,16},{16,24},{24,32},{32,40},{40,48},{48,56},{56,64},{64,7... | collective-permute-start | bytes 786440 | tf_op jit(solution)/shard_map/ppermute | solution.py:18
  54.3 5.4 %copy-start.10 = (bf16[512,256]{0,1:T(8,128)(2,1)S(1)}, bf16[512,256]{0,1:T(8,128)(2,1)}, u32[]{:S(2)}) copy-start(bf16[512,256]{0,1:T(8,128)(2,1)} %copy-done.9) | copy-start | bytes 786436
  55.9 3.9 copy-start.7
  81.2 1.8 copy-start.14
  81.2 2.5 copy-start.2
  81.2 98.2 %all-gather.6.cloned.1.call-start = ((), (), s32[]{:S(2)}) async-start(), calls=%async_computation.7 | async-start | bytes 5947392 | tf_op jit(solution)/shard_map/all_gather | solution.py:115
  81.8 183.8 %all-gather.4.cloned.1.call-start = ((), (), s32[]{:S(2)}) async-start(), calls=%async_computation.6 | async-start | bytes 5947392 | tf_op jit(solution)/shard_map/all_gather | solution.py:114
  82.4 269.4 %all-gather.8.cloned.1.call-start = ((), (), s32[]{:S(2)}) async-start(), calls=%async_computation.8 | async-start | bytes 5947392 | tf_op jit(solution)/shard_map/all_gather | solution.py:116
  85.2 42.7 %copy-start.12 = (bf16[64,2048]{1,0:T(8,128)(2,1)S(1)}, bf16[64,2048]{1,0:T(8,128)(2,1)}, u32[]{:S(2)}) copy-start(bf16[64,2048]{1,0:T(8,128)(2,1)} %param.16) | copy-start | bytes 786436
  85.2 43.8 %copy-start.13 = (f32[2048]{0:T(1024)S(1)}, f32[2048]{0:T(1024)}, u32[]{:S(2)}) copy-start(f32[2048]{0:T(1024)} %param.21) | copy-start | bytes 24580
  133.3 16.6 %all-to-all-start = ((bf16[8,18,2048]{2,1,0:T(8,128)(2,1)}), bf16[8,18,2048]{2,1,0:T(8,128)(2,1)S(1)}, u32[]{:S(2)}, u32[]{:S(2)}) async-start(bf16[8,18,2048]{2,1,0:T(8,128)(2,1)} %reshape.194), calls=%async_computation.1 | async-start | bytes 1572864 | tf_op jit(solution)/shard_map/all_to_all | solution.py:118
  149.9 0.9 copy-start.5
  150.8 207.4 %all-to-all-start.2 = ((bf16[8,18,2048]{2,1,0:T(8,128)(2,1)}), bf16[8,18,2048]{2,1,0:T(8,128)(2,1)S(1)}, u32[]{:S(2)}, u32[]{:S(2)}) async-start(bf16[8,18,2048]{2,1,0:T(8,128)(2,1)} %reshape.200), calls=%async_computation.3 | async-start | bytes 1572864 | tf_op jit(solution)/shard_map/all_to_all | solution.py:119
  154.4 111.3 %copy-start.6 = (bf16[8,18,2048]{2,1,0:T(8,128)(2,1)S(1)}, bf16[8,18,2048]{2,1,0:T(8,128)(2,1)}, u32[]{:S(2)}) copy-start(bf16[8,18,2048]{2,1,0:T(8,128)(2,1)} %copy-done.5) | copy-start | bytes 1769476
  358.2 17.4 %all-to-all-start.1 = ((bf16[8,18,2048]{2,1,0:T(8,128)(2,1)}), bf16[8,18,2048]{2,1,0:T(8,128)(2,1)S(1)}, u32[]{:S(2)}, u32[]{:S(2)}) async-start(bf16[8,18,2048]{2,1,0:T(8,128)(2,1)} %fusion.35), calls=%async_computation.2 | async-start | bytes 1572864 | tf_op jit(solution)/shard_map/all_to_all | solution.py:150
  362.5 4.2 %copy-start.17 = (f32[8,1,18,1408]{3,2,0,1:T(8,128)S(1)}, f32[8,1,18,1408]{3,2,0,1:T(8,128)}, u32[]{:S(2)}) copy-start(f32[8,1,18,1408]{3,2,0,1:T(8,128)} %fusion.20) | copy-start | bytes 2433028
  362.5 9.2 %slice-start = ((s8[5767168]{0:T(1024)(128)(4,1)}), s8[4194304]{0:T(1024)(128)(4,1)S(1)}, s32[]{:S(2)}) async-start(s8[5767168]{0:T(1024)(128)(4,1)} %bitcast.109), calls=%async_computation.9 | async-start | bytes 8388608
  366.7 5.0 %slice-start.1 = ((s8[5767168]{0:T(1024)(128)(4,1)}), s8[1572864]{0:T(1024)(128)(4,1)S(1)}, s32[]{:S(2)}) async-start(s8[5767168]{0:T(1024)(128)(4,1)} %bitcast.109), calls=%async_computation.10 | async-start | bytes 3145728
  366.7 5.0 %copy-start.16 = (f32[8,1,18,1408]{3,2,0,1:T(8,128)S(1)}, f32[8,1,18,1408]{3,2,0,1:T(8,128)}, u32[]{:S(2)}) copy-start(f32[8,1,18,1408]{3,2,0,1:T(8,128)} %fusion.23) | copy-start | bytes 2433028
  374.9 5.2 %copy-start.15 = (f32[64,2]{0,1:T(2,128)S(1)}, f32[64,2]{0,1:T(2,128)}, u32[]{:S(2)}) copy-start(f32[64,2]{0,1:T(2,128)} %param.26) | copy-start | bytes 1540
  375.7 17.5 %all-to-all-start.3 = ((bf16[8,18,2048]{2,1,0:T(8,128)(2,1)}), bf16[8,18,2048]{2,1,0:T(8,128)(2,1)}, u32[]{:S(2)}, u32[]{:S(2)}) async-start(bf16[8,18,2048]{2,1,0:T(8,128)(2,1)} %fusion.32), calls=%async_computation.4 | async-start | bytes 1572864 | tf_op jit(solution)/shard_map/all_to_all | solution.py:151
  401.6 5.4 %copy-start.1 = (f32[128,2048]{1,0:T(8,128)S(1)}, f32[128,2048]{1,0:T(8,128)}, u32[]{:S(2)}) copy-start(f32[128,2048]{1,0:T(8,128)} %mul.154) | copy-start | bytes 3145732
  406.7 1.3 copy-start.3
  406.7 1.3 copy-start.4
Sparse Core Ops, SparseCore 0:
  81.4 46.4 reduce-scatter.1
Sparse Core Ops, SparseCore 1:
  84.3 95.1 all-gather.5
  181.9 83.7 all-gather.3
  268.1 83.7 all-gather.7
where the time goes:
time: 420 us; the launch traced here: 417 us
  waiting for transfers between devices  266 us (63%)
  matrix products  50.4 us (12%)
  starting transfers between devices  43.9 us (10%)
  local copies, waits for them, and re-layouts  25.7 us (6%)
  between operations  16.2 us (4%)
  other arithmetic  14 us (3%)
    all_gather x1, waiting for transfers between devices, per_device(): lax.all_gather(w_down, 'seq', axis=2, tiled=True)  81.2 us
    all_gather x1, waiting for transfers between devices, per_device(): lax.all_gather(w_gate, 'seq', axis=1, tiled=True)  80.9 us
    reduce_scatter x1, waiting for transfers between devices, per_device(): lax.psum_scatter(jnp.dot(attn, w_out, preferred_element_type=jnp.float32)...  41.6 us
    ppermute x8, starting transfers between devices, from_behind(): return lax.ppermute(block, axis, route)  27.9 us
    all_gather x1, waiting for transfers between devices, per_device(): lax.all_gather(w_up, 'seq', axis=1, tiled=True)  25 us
    ppermute x8, waiting for transfers between devices, from_behind(): return lax.ppermute(block, axis, route)  14.8 us
    all_to_all x1, waiting for transfers between devices, per_device(): lax.all_to_all(send_in, 'exp', split_axis=0, concat_axis=0, tiled=True)  12 us
    dot_general x1, matrix products, window_attention(): jnp.einsum('hqk,khd->qhd', weights, val_heads, preferred_element_type=jnp...  8.68 us
  transfers between devices with their start and end apart: 16, of which 14 were waited for; matrix products, arithmetic and copies ran while one was open for 12% of the time, Pallas kernels for 0%

commit v1 on v0

v1 whole, which is shorter than its diff:
```python
import functools
import math

import jax
import jax.numpy as jnp
from jax import lax
from jax.experimental import pallas as pl
from jax.experimental.pallas import tpu as pltpu
from jax.sharding import PartitionSpec as P

HD = 128
W = 2048
CAP = 18
SLOT = 24
NZ = 8
NX = 4
NY = 4
norm_eps = 1e-06
F32 = jnp.float32
BF16 = jnp.bfloat16
VMEM = pl.BlockSpec(memory_space=pltpu.VMEM)
ANY = pl.BlockSpec(memory_space=pl.ANY)


def params(mib):
    return pltpu.CompilerParams(vmem_limit_bytes=mib * 2**20)


def nt(a, b):
    return lax.dot_general(a, b, (((1,), (1,)), ((), ())), preferred_element_type=F32)


def nn(a, b):
    return jnp.dot(a, b, preferred_element_type=F32)


def from_behind(block, axis, distance):
    devices = range(lax.axis_size(axis))
    route = [(i - distance, i) for i in devices if i - distance in devices]
    return lax.ppermute(block, axis, route)


def shift_y(block, d):
    return lax.ppermute(block, "exp", [(i, (i + 2 * d) % (2 * NY)) for i in range(2 * NY)])


def swap_core(block):
    return lax.ppermute(block, "exp", [(i, i ^ 1) for i in range(2 * NY)])


def window_attention(queries, key_rows, val_rows, seq_base):
    tok_seq = queries.shape[0]
    feat_width = queries.shape[1]
    head_count = feat_width // HD
    key_span = key_rows.shape[0]
    reach_len = key_span - tok_seq
    key_heads = key_rows.reshape(key_span, head_count, HD)
    val_heads = val_rows.reshape(key_span, head_count, HD)
    score_scale = 1.0 / math.sqrt(HD)
    key_pos = seq_base - reach_len + jnp.arange(key_span, dtype=jnp.int32)
    query_heads = queries.reshape(tok_seq, head_count, HD)
    scores = jnp.einsum("qhd,khd->hqk", query_heads, key_heads, preferred_element_type=F32) * score_scale
    query_pos = seq_base + jnp.arange(tok_seq, dtype=jnp.int32)
    offset = query_pos[:, None] - key_pos[None, :]
    allowed = (offset >= 0) & (offset < reach_len) & (key_pos[None, :] >= 0)
    scores = jnp.where(allowed[None], scores, -jnp.inf)
    row_max = jnp.max(scores, axis=-1, keepdims=True)
    exp_scores = jnp.exp(scores - row_max)
    weights = (exp_scores / jnp.sum(exp_scores, axis=-1, keepdims=True)).astype(BF16)
    mixed = jnp.einsum("hqk,khd->qhd", weights, val_heads, preferred_element_type=F32)
    return mixed.reshape(tok_seq, feat_width).astype(BF16)


def project_kernel(where, own, sib, w_own, w_sib, out):
    for d in range(NY):
        y = lax.rem(where[0] + d, NY)
        out[d] = (nn(own[y], w_own[...]) + nn(sib[y], w_sib[...])).astype(BF16)


def project(where, own, sib, w_own, w_sib):
    return pl.pallas_call(
        project_kernel,
        out_shape=jax.ShapeDtypeStruct((NY, own.shape[1], w_own.shape[1]), BF16),
        in_specs=[pl.BlockSpec(memory_space=pltpu.SMEM)] + [VMEM] * 4,
        out_specs=VMEM,
        compiler_params=params(24),
        cost_estimate=pl.CostEstimate(flops=2 * 256 * 512 * 2048, bytes_accessed=6 * 2**20, transcendentals=0),
    )(where, own, sib, w_own, w_sib)


def slots_of(target_rows, slots, tokens):
    at = lax.broadcasted_iota(jnp.int32, (slots, tokens), 0)
    hit = (at == target_rows[0:1, :]) | (at == target_rows[1:2, :])
    return jnp.where(hit, 1.0, 0.0).astype(BF16)


def norm_kernel(x, p0, p1, p2, p3, gain, target_rows, hidden, send):
    total = p0[...].astype(F32) + p1[...].astype(F32) + p2[...].astype(F32) + p3[...].astype(F32)
    state = (x[...].astype(F32) + total).astype(BF16)
    hidden[...] = state
    wide = state.astype(F32)
    rstd = lax.rsqrt(jnp.mean(wide * wide, axis=-1, keepdims=True) + norm_eps)
    moe_in = (wide * rstd * gain[...]).astype(BF16)
    place = slots_of(target_rows, send.shape[0], x.shape[0])
    send[...] = nn(place, moe_in).astype(BF16)


def norm_dispatch(x, parts, gain, target_rows, slots):
    tokens, width = x.shape
    return pl.pallas_call(
        norm_kernel,
        out_shape=(
            jax.ShapeDtypeStruct((tokens, width), BF16),
            jax.ShapeDtypeStruct((slots, width), BF16),
        ),
        in_specs=[VMEM] * 7,
        out_specs=(VMEM, VMEM),
        compiler_params=params(24),
        cost_estimate=pl.CostEstimate(flops=2 * slots * tokens * width, bytes_accessed=3 * 2**20, transcendentals=0),
    )(x, *parts, gain, target_rows)


def scatter_kernel(rows, target_rows, send):
    place = slots_of(target_rows, send.shape[0], rows.shape[0])
    send[...] = nn(place, rows[...]).astype(BF16)


def scatter_rows(rows, target_rows, slots):
    return pl.pallas_call(
        scatter_kernel,
        out_shape=jax.ShapeDtypeStruct((slots, rows.shape[1]), BF16),
        in_specs=[VMEM] * 2,
        out_specs=VMEM,
        compiler_params=params(16),
        cost_estimate=pl.CostEstimate(flops=2 * slots * 64 * 2048, bytes_accessed=2**20, transcendentals=0),
    )(rows, target_rows)


def expert_kernel(part, rows_in, rows_grad, chunk, out, back, wg, wu, wd, ga, ua, ba, hid, gpg, gpu, sems):
    shards = chunk.shape[0]
    mats = (wg, wu, wd)
    group = 4
    steps = shards // group
    span = group * part

    def start(s, _):
        for m in range(3):
            pltpu.make_async_copy(
                chunk.at[s, pl.ds(m * part, part)], mats[m].at[pl.ds(s * part, part)], sems.at[m, s // group]
            ).start()
        return 0

    lax.fori_loop(0, shards, start, 0)

    def wait(m, k):
        view = mats[m].at[pl.ds(k * span, span)]
        pltpu.make_async_copy(view, view, sems.at[m, k]).wait()

    for k in range(steps):
        cols = pl.ds(k * span, span)
        for m, (rows, acc) in enumerate(((rows_in, ga), (rows_in, ua), (rows_grad, ba))):
            wait(m, k)
            term = nn(rows[:, cols], mats[m][cols, :])
            acc[...] = term if k == 0 else acc[...] + term

    def point(i, _):
        r = pl.ds(pl.multiple_of(i * 16, 16), 16)
        gate, up, grad = ga[r, :], ua[r, :], ba[r, :]
        sigma = jax.nn.sigmoid(gate)
        act = gate * sigma
        hid[r, :] = (act * up).astype(BF16)
        gpg[r, :] = (grad * up * sigma * (1.0 + gate * (1.0 - sigma))).astype(BF16)
        gpu[r, :] = (grad * act).astype(BF16)
        return 0

    lax.fori_loop(0, hid.shape[0] // 16, point, 0)

    def finish(k, _):
        cols = pl.ds(pl.multiple_of(k * span, span), span)
        out[:, cols] = nt(hid[...], wd[cols, :]).astype(BF16)
        back[:, cols] = (nt(gpg[...], wg[cols, :]) + nt(gpu[...], wu[cols, :])).astype(BF16)
        return 0

    lax.fori_loop(0, steps, finish, 0)


def experts(rows_in, rows_grad, chunk):
    rows, width = rows_in.shape
    shards, depth, hidden = chunk.shape
    part = depth // 3
    made = jax.ShapeDtypeStruct((rows, width), BF16)
    return pl.pallas_call(
        functools.partial(expert_kernel, part),
        out_shape=(made, made),
        in_specs=[VMEM, VMEM, ANY],
        out_specs=(VMEM, VMEM),
        scratch_shapes=[pltpu.VMEM((width, hidden), BF16)] * 3
        + [pltpu.VMEM((rows, hidden), F32)] * 3
        + [pltpu.VMEM((rows, hidden), BF16)] * 3
        + [pltpu.SemaphoreType.DMA((3, shards // 4))],
        compiler_params=params(40),
        cost_estimate=pl.CostEstimate(
            flops=12 * rows * width * hidden, bytes_accessed=20 * 2**20, transcendentals=rows * hidden
        ),
    )(rows_in, rows_grad, chunk)


def combine_kernel(hidden, grad_out, row_out, row_back, target, prob, gain, layer_out, grad_in, grad_gate):
    tokens = hidden.shape[0]
    slots = row_out.shape[0]
    at = lax.broadcasted_iota(jnp.int32, (tokens, slots), 1)
    pick = [jnp.where(at == target[:, c : c + 1], 1.0, 0.0).astype(BF16) for c in (0, 1)]
    wide = hidden[...].astype(F32)
    grad = grad_out[...].astype(F32)
    out0, out1 = nn(pick[0], row_out[...]), nn(pick[1], row_out[...])
    p0, p1 = prob[:, 0:1], prob[:, 1:2]
    layer_out[...] = (wide + (p0 * out0 + p1 * out1)).astype(BF16)
    grad_gate[:, 0:1] = jnp.sum(grad * out0, axis=-1, keepdims=True)
    grad_gate[:, 1:2] = jnp.sum(grad * out1, axis=-1, keepdims=True)
    moe_grad = p0 * nn(pick[0], row_back[...]) + p1 * nn(pick[1], row_back[...])
    rstd = lax.rsqrt(jnp.mean(wide * wide, axis=-1, keepdims=True) + norm_eps)
    normed = wide * rstd
    scaled = moe_grad * gain[...]
    mean = jnp.mean(scaled * normed, axis=-1, keepdims=True)
    grad_in[...] = (grad + rstd * (scaled - normed * mean)).astype(BF16)


def combine(hidden, grad_out, row_out, row_back, target, prob, gain):
    tokens, width = hidden.shape
    made = jax.ShapeDtypeStruct((tokens, width), BF16)
    return pl.pallas_call(
        combine_kernel,
        out_shape=(made, made, jax.ShapeDtypeStruct((tokens, 2), F32)),
        in_specs=[VMEM] * 7,
        out_specs=(VMEM,) * 3,
        compiler_params=params(24),
        cost_estimate=pl.CostEstimate(flops=2**28, bytes_accessed=3 * 2**20, transcendentals=0),
    )(hidden, grad_out, row_out, row_back, target, prob, gain)


def per_device(
    x_resid, queries, key_proj, val_proj, w_out, norm_gain, w_gate, w_up, w_down, routes, gate_prob, grad_out
):
    tok_seq = queries.shape[0]
    tok_dev, width = x_resid.shape
    me_exp = lax.axis_index("exp")
    core, y = me_exp % 2, me_exp // 2
    stacked = jnp.concatenate([w_gate[0], w_up[0], w_down[0].T], axis=0)
    chunk = lax.all_gather(stacked, "seq", axis=0)

    flat = routes.reshape(-1)
    order = jnp.arange(flat.shape[0], dtype=jnp.int32)
    same = (flat[:, None] == flat[None, :]) & (order[None, :] < order[:, None])
    rank = jnp.sum(same.astype(jnp.int32), axis=1)
    target = (flat * SLOT + rank).reshape(tok_dev, 2)
    target_rows = target.T
    slots = 2 * NY * SLOT
    gain = norm_gain[None, :]

    def exchange(rows):
        return lax.all_to_all(
            rows.reshape(2 * NY, SLOT, width), "exp", split_axis=0, concat_axis=0, tiled=True
        ).reshape(slots, width)

    recv_grad = exchange(scatter_rows(grad_out, target_rows, slots))
    w_sib = swap_core(w_out)

    hop_count = W // tok_seq
    seq_base = lax.axis_index("seq") * tok_seq
    earlier = []
    carried = (key_proj, val_proj)
    for _ in range(hop_count):
        carried = from_behind(carried, "seq", 1)
        earlier.insert(0, carried)
    key_rows = jnp.concatenate([pair[0] for pair in earlier] + [key_proj], axis=0)
    val_rows = jnp.concatenate([pair[1] for pair in earlier] + [val_proj], axis=0)
    attn = window_attention(queries, key_rows, val_rows, seq_base)

    owners = attn.reshape(NY, 2, tok_dev, attn.shape[1])
    mine = lax.dynamic_index_in_dim(owners, core, 1, keepdims=False)
    theirs = swap_core(lax.dynamic_index_in_dim(owners, 1 - core, 1, keepdims=False))
    partial = project(y[None].astype(jnp.int32), mine, theirs, w_out, w_sib)
    parts = [partial[0]] + [shift_y(partial[d], d) for d in (1, 2, 3)]
    hidden, send_in = norm_dispatch(x_resid, parts, gain, target_rows, slots)
    recv_in = exchange(send_in)
    out_rows, back_rows = experts(recv_in, recv_grad, chunk)
    return combine(hidden, grad_out, exchange(out_rows), exchange(back_rows), target, gate_prob, gain)


def solution(mesh):
    tokens = P(("seq", "exp"), None)
    heads = P("seq", "exp")
    placed = (
        tokens,
        heads,
        heads,
        heads,
        P("exp", None),
        P(),
        P("exp", "seq", None),
        P("exp", "seq", None),
        P("exp", None, "seq"),
        tokens,
        tokens,
        tokens,
    )
    return jax.shard_map(
        per_device, mesh=mesh, in_specs=placed, out_specs=(tokens, tokens, tokens), check_vma=False
    )
```

time: 420 us -> 235 us (0.56)
  waiting for transfers between devices: 266 us -> 65.3 us
  blocking collectives: 0 us -> 33 us
  matrix products: 50.4 us -> 21.4 us
  Pallas kernels: 0 us -> 24 us
  other arithmetic: 14 us -> 5.31 us
  local copies, waits for them, and re-layouts: 25.7 us -> 17.6 us
  starting transfers between devices: 43.9 us -> 50 us
    all_gather x3 -> x1, waiting for transfers between devices: 187 us -> 14.9 us  [per_device(): chunk = lax.all_gather(stacked, 'seq', axis=0)]
    reduce_scatter x1 -> x0, waiting for transfers between devices: 41.6 us -> none  [per_device(): lax.psum_scatter(jnp.dot(attn, w_out, preferred_element_type=jnp.float32)...]
    all_to_all x0 -> x2, blocking collectives: none -> 33 us  [exchange(): lax.all_to_all(rows.reshape(2 * NY, SLOT, width), 'exp', split_axis=0, co...]
    dot_general x8 -> x1, matrix products: 39.8 us -> 8.79 us  [window_attention(): jnp.einsum('hqk,khd->qhd', weights, val_heads, preferred_element_type=F32)]
    pallas_call x0 -> x5, Pallas kernels: none -> 24 us  [the longest x1 18.9 us: experts(): pl.pallas_call(functools.partial(expert_kernel, part), out_shape=(made, m...]
    ppermute x0 -> x5, waiting for transfers between devices: none -> 16.5 us  [the longest x3 16.5 us: shift_y(): lax.ppermute(block, 'exp', [(i, (i + 2 * d) % (2 * NY)) for i in range(2...]
    all_to_all x4 -> x2, waiting for transfers between devices: 21.4 us -> 13 us  [exchange(): lax.all_to_all(rows.reshape(2 * NY, SLOT, width), 'exp', split_axis=0, co...]
    all_to_all x4 -> x2, starting transfers between devices: 15.8 us -> 7.98 us  [exchange(): lax.all_to_all(rows.reshape(2 * NY, SLOT, width), 'exp', split_axis=0, co...]
  transfers between devices with their start and end apart: 16 -> 16, of which waited for: 14 -> 9; matrix products, arithmetic and copies ran while one was open for 12% -> 18% of each run, Pallas kernels for 0% -> 1%
where the time goes in v1:
time: 235 us; the launch traced here: 231 us
  waiting for transfers between devices  65.3 us (28%)
  starting transfers between devices  50 us (21%)
  blocking collectives  33 us (14%)
  Pallas kernels  24 us (10%)
  matrix products  21.4 us (9%)
  local copies, waits for them, and re-layouts  17.6 us (7%)
  between operations  14.4 us (6%)
  other arithmetic  5.31 us (2%)
    ppermute x8, starting transfers between devices, from_behind(): return lax.ppermute(block, axis, route)  35.6 us
    all_to_all x2, blocking collectives, exchange(): lax.all_to_all(rows.reshape(2 * NY, SLOT, width), 'exp', split_axis=0, co...  33 us
    ppermute x8, waiting for transfers between devices, from_behind(): return lax.ppermute(block, axis, route)  20.9 us
    pallas_call x1, Pallas kernels, experts(): pl.pallas_call(functools.partial(expert_kernel, part), out_shape=(made, m...  18.9 us
    ppermute x3, waiting for transfers between devices, shift_y(): lax.ppermute(block, 'exp', [(i, (i + 2 * d) % (2 * NY)) for i in range(2...  16.5 us
    all_gather x1, waiting for transfers between devices, per_device(): chunk = lax.all_gather(stacked, 'seq', axis=0)  14.9 us
    all_to_all x2, waiting for transfers between devices, exchange(): lax.all_to_all(rows.reshape(2 * NY, SLOT, width), 'exp', split_axis=0, co...  13 us
    unnamed x29, local copies, waits for them, and re-layouts  12.1 us
  transfers between devices with their start and end apart: 16, of which 9 were waited for; matrix products, arithmetic and copies ran while one was open for 18% of the time, Pallas kernels for 1%

profile of v1, /device:TPU:2, one launch (start us, length us, event | category | flops | bytes accessed | tf_op | source)
XLA Modules:
  0.0 231.1 jit_solution(2229901718116552570)
XLA Ops:
  7.3 2.1 pad_maximum_fusion
  9.4 3.4 %collective-permute-start = (bf16[512,256]{1,0:T(8,128)(2,1)S(1)}, bf16[512,256]{1,0:T(8,128)(2,1)S(1)}, u32[]{:S(2)}, u32[]{:S(2)}) collective-permute-start(bf16[512,256]{1,0:T(8,128)(2,1)S(1)} %copy-done.6), channel_id=1, source_target_pairs={{0,8},{8,16},{16,24},{24,32},{32,40},{40,48},{48,56},{56,64},{64,7... | collective-permute-start | bytes 786440 | tf_op jit(solution)/shard_map/ppermute | solution.py:40
  12.9 3.1 %collective-permute-start.4 = (bf16[512,256]{0,1:T(8,128)(2,1)S(1)}, bf16[512,256]{0,1:T(8,128)(2,1)S(1)}, u32[]{:S(2)}, u32[]{:S(2)}) collective-permute-start(bf16[512,256]{0,1:T(8,128)(2,1)S(1)} %copy.56), channel_id=1, source_target_pairs={{0,8},{8,16},{16,24},{24,32},{32,40},{40,48},{48,56},{56,64},{64,7... | collective-permute-start | bytes 786440 | tf_op jit(solution)/shard_map/ppermute | solution.py:40
  16.1 4.4 %collective-permute-done = bf16[512,256]{1,0:T(8,128)(2,1)S(1)} collective-permute-done((bf16[512,256]{1,0:T(8,128)(2,1)S(1)}, bf16[512,256]{1,0:T(8,128)(2,1)S(1)}, u32[]{:S(2)}, u32[]{:S(2)}) %collective-permute-start) | collective-permute-done | bytes 262176 | tf_op jit(solution)/shard_map/ppermute | solution.py:40
  20.5 3.4 %collective-permute-start.1 = (bf16[512,256]{1,0:T(8,128)(2,1)S(1)}, bf16[512,256]{1,0:T(8,128)(2,1)}, u32[]{:S(2)}, u32[]{:S(2)}) collective-permute-start(bf16[512,256]{1,0:T(8,128)(2,1)S(1)} %collective-permute-done), channel_id=1, source_target_pairs={{0,8},{8,16},{16,24},{24,32},{32,40},{40,48},{48,56},{56,64},{64,7... | collective-permute-start | bytes 786440 | tf_op jit(solution)/shard_map/ppermute | solution.py:40
  24.0 2.1 collective-permute-done.4
  26.1 3.4 %collective-permute-start.5 = (bf16[512,256]{0,1:T(8,128)(2,1)S(1)}, bf16[512,256]{0,1:T(8,128)(2,1)}, u32[]{:S(2)}, u32[]{:S(2)}) collective-permute-start(bf16[512,256]{0,1:T(8,128)(2,1)S(1)} %collective-permute-done.4), channel_id=1, source_target_pairs={{0,8},{8,16},{16,24},{24,32},{32,40},{40,48},{48,56},{56,64},{64,7... | collective-permute-start | bytes 786440 | tf_op jit(solution)/shard_map/ppermute | solution.py:40
  29.5 6.0 %collective-permute-done.1 = bf16[512,256]{1,0:T(8,128)(2,1)} collective-permute-done((bf16[512,256]{1,0:T(8,128)(2,1)S(1)}, bf16[512,256]{1,0:T(8,128)(2,1)}, u32[]{:S(2)}, u32[]{:S(2)}) %collective-permute-start.1) | collective-permute-done | bytes 262176 | tf_op jit(solution)/shard_map/ppermute | solution.py:40
  35.5 3.3 %collective-permute-start.2 = (bf16[512,256]{1,0:T(8,128)(2,1)}, bf16[512,256]{1,0:T(8,128)(2,1)}, u32[]{:S(2)}, u32[]{:S(2)}) collective-permute-start(bf16[512,256]{1,0:T(8,128)(2,1)} %collective-permute-done.1), channel_id=1, source_target_pairs={{0,8},{8,16},{16,24},{24,32},{32,40},{40,48},{48,56},{56,64},{64,7... | collective-permute-start | bytes 786440 | tf_op jit(solution)/shard_map/ppermute | solution.py:40
  38.8 5.2 %collective-permute-done.5 = bf16[512,256]{0,1:T(8,128)(2,1)} collective-permute-done((bf16[512,256]{0,1:T(8,128)(2,1)S(1)}, bf16[512,256]{0,1:T(8,128)(2,1)}, u32[]{:S(2)}, u32[]{:S(2)}) %collective-permute-start.5) | collective-permute-done | bytes 262176 | tf_op jit(solution)/shard_map/ppermute | solution.py:40
  44.1 4.5 %collective-permute-start.6 = (bf16[512,256]{0,1:T(8,128)(2,1)}, bf16[512,256]{0,1:T(8,128)(2,1)}, u32[]{:S(2)}, u32[]{:S(2)}) collective-permute-start(bf16[512,256]{0,1:T(8,128)(2,1)} %collective-permute-done.5), channel_id=1, source_target_pairs={{0,8},{8,16},{16,24},{24,32},{32,40},{40,48},{48,56},{56,64},{64,7... | collective-permute-start | bytes 786440 | tf_op jit(solution)/shard_map/ppermute | solution.py:40
  48.5 3.2 %collective-permute-done.2 = bf16[512,256]{1,0:T(8,128)(2,1)} collective-permute-done((bf16[512,256]{1,0:T(8,128)(2,1)}, bf16[512,256]{1,0:T(8,128)(2,1)}, u32[]{:S(2)}, u32[]{:S(2)}) %collective-permute-start.2) | collective-permute-done | bytes 262176 | tf_op jit(solution)/shard_map/ppermute | solution.py:40
  51.7 3.4 %collective-permute-start.3 = (bf16[512,256]{1,0:T(8,128)(2,1)}, bf16[512,256]{1,0:T(8,128)(2,1)}, u32[]{:S(2)}, u32[]{:S(2)}) collective-permute-start(bf16[512,256]{1,0:T(8,128)(2,1)} %collective-permute-done.2), channel_id=1, source_target_pairs={{0,8},{8,16},{16,24},{24,32},{32,40},{40,48},{48,56},{56,64},{64,7... | collective-permute-start | bytes 786440 | tf_op jit(solution)/shard_map/ppermute | solution.py:40
  55.1 3.0 %fusion.5 = pred[512,2560]{0,1:T(8,128)(4,1)} fusion(s32[2560]{0:T(1024)S(1)} %iota_add_fusion, s32[512]{0:T(512)S(1)} %iota_add_fusion.1, pred[2560]{0:T(1024)(128)(4,1)S(1)} %broadcast_compare_fusion), kind=kLoop, calls=%fused_computation.10 | loop fusion | flops 6553600 | bytes 1325568 | tf_op jit(solution)/shard_map/and | solution.py:65
  58.1 11.1 %collective-permute-start.7 = (bf16[512,256]{0,1:T(8,128)(2,1)}, bf16[512,256]{0,1:T(8,128)(2,1)}, u32[]{:S(2)}, u32[]{:S(2)}) collective-permute-start(bf16[512,256]{0,1:T(8,128)(2,1)} %collective-permute-done.6), channel_id=1, source_target_pairs={{0,8},{8,16},{16,24},{24,32},{32,40},{40,48},{48,56},{56,64},{64,7... | collective-permute-start | bytes 786440 | tf_op jit(solution)/shard_map/ppermute | solution.py:40
  69.3 1.7 constant_dynamic-update-slice_fusion.4
  71.0 1.7 constant_dynamic-update-slice_fusion.3
  72.6 1.7 constant_dynamic-update-slice_fusion.2
  74.3 0.7 constant_dynamic-update-slice_fusion.1
  75.0 0.7 constant_dynamic-update-slice_fusion
  75.7 2.5 %copy.55 = bf16[2560,256]{0,1:T(8,128)(2,1)} copy(bf16[2560,256]{1,0:T(8,128)(2,1)} %constant_dynamic-update-slice_fusion) | data formatting | bytes 2621440 | tf_op jit(solution)/shard_map/concatenate | solution.py:276
  78.2 1.7 constant_dynamic-update-slice_fusion.9
  79.9 1.7 constant_dynamic-update-slice_fusion.8
  81.6 1.7 constant_dynamic-update-slice_fusion.7
  83.3 0.8 constant_dynamic-update-slice_fusion.6
  84.0 0.8 constant_dynamic-update-slice_fusion.5
  84.8 5.7 %fusion.26 = f32[2,512]{1,0:T(2,128)S(1)} fusion(pred[512,2560]{0,1:T(8,128)(4,1)} %fusion.5, bf16[2560,2,128]{0,2,1:T(8,128)(2,1)} %bitcast.2, bf16[512,256]{1,0:T(8,128)(2,1)S(1)} %copy-done), kind=kOutput, calls=%fused_computation.49 | convolution fusion | flops 681576960 | bytes 2887680 | tf_op jit(solution)/shard_map/sub | solution.py:68
  90.5 6.9 %fusion.14 = f32[2,2560,512]{2,1,0:T(8,128)} fusion(bf16[2560,2,128]{0,2,1:T(8,128)(2,1)} %bitcast.2, bf16[512,256]{1,0:T(8,128)(2,1)S(1)} %copy-done), kind=kOutput, calls=%fused_computation.18 | convolution fusion | flops 671088640 | bytes 12058624 | tf_op jit(solution)/shard_map/qhd,khd->hqk/dot_general | solution.py:62
  97.5 8.8 %fusion.9 = bf16[512,2,128]{0,2,1:T(8,128)(2,1)S(1)} fusion(bf16[2560,2,128]{0,2,1:T(8,128)(2,1)} %bitcast.71, f32[2,512]{1,0:T(2,128)S(1)} %fusion.26, f32[2,2560,512]{2,1,0:T(8,128)} %fusion.14, pred[512,2560]{0,1:T(8,128)(4,1)} %fusion.5), kind=kOutput, calls=%fused_computation.14 | convolution fusion | flops 684330496 | bytes 13373440 | tf_op jit(solution)/shard_map/hqk,khd->qhd/dot_general | solution.py:70
  106.8 0.2 copy-done.7
  107.3 0.2 convert_reduce_fusion
  107.7 1.2 shard_map.141
  108.9 4.4 %all-to-all-start.1 = ((bf16[8,24,2048]{2,1,0:T(8,128)(2,1)}), bf16[8,24,2048]{2,1,0:T(8,128)(2,1)}, u32[]{:S(2)}, u32[]{:S(2)}) async-start(bf16[8,24,2048]{2,1,0:T(8,128)(2,1)} %bitcast.15), calls=%async_computation.1 | async-start | bytes 1572864 | tf_op jit(solution)/shard_map/all_to_all | solution.py:261
  113.4 1.6 shard_map.139
  115.1 2.1 collective-permute-start.10
  117.2 2.7 %collective-permute-start.11 = (bf16[64,2048]{1,0:T(8,128)(2,1)S(1)}, bf16[64,2048]{1,0:T(8,128)(2,1)S(1)}, u32[]{:S(2)}, u32[]{:S(2)}) collective-permute-start(bf16[64,2048]{1,0:T(8,128)(2,1)S(1)} %get-tuple-element.24), channel_id=1, source_target_pairs={{0,4},{1,5},{2,6},{3,7},{4,0},{5,1},{6,2},{7,3},{8,12},{9,13},{10,... | collective-permute-start | bytes 786440 | tf_op jit(solution)/shard_map/ppermute | solution.py:44
  119.9 1.5 collective-permute-start.12
  121.3 10.7 %collective-permute-done.10.p1 = bf16[64,2048]{1,0:T(8,128)(2,1)S(1)} collective-permute-done((bf16[64,2048]{1,0:T(8,128)(2,1)S(1)}, bf16[64,2048]{1,0:T(8,128)(2,1)S(1)}, u32[]{:S(2)}, u32[]{:S(2)}) %collective-permute-start.10) | collective-permute-done | bytes 262176 | tf_op jit(solution)/shard_map/ppermute | solution.py:44
  132.0 5.8 %collective-permute-done.11.p2 = bf16[64,2048]{1,0:T(8,128)(2,1)S(1)} collective-permute-done((bf16[64,2048]{1,0:T(8,128)(2,1)S(1)}, bf16[64,2048]{1,0:T(8,128)(2,1)S(1)}, u32[]{:S(2)}, u32[]{:S(2)}) %collective-permute-start.11) | collective-permute-done | bytes 262176 | tf_op jit(solution)/shard_map/ppermute | solution.py:44
  137.8 0.6 shard_map.140
  138.5 15.7 %all_to_all.20 = bf16[8,24,2048]{2,1,0:T(8,128)(2,1)S(1)} all-to-all(bf16[8,24,2048]{2,1,0:T(8,128)(2,1)S(1)} %bitcast.65), channel_id=1, replica_groups=mesh['seq'=32,'exp'=8] {'exp'}, dimensions={0} | all-to-all | bytes 1572864 | tf_op jit(solution)/shard_map/all_to_all | solution.py:261
  154.1 14.9 %all-gather.3.cloned.1.call-done = bf16[6144,1408]{1,0:T(8,128)(2,1)} async-done(((bf16[192,1408]{1,0:T(8,128)(2,1)}), bf16[6144,1408]{1,0:T(8,128)(2,1)}) %all-gather.3.cloned.1.call-update) | async-done | bytes 17301520 | tf_op jit(solution)/shard_map/all_gather | solution.py:249
  169.0 18.9 %shard_map.142 = (bf16[192,2048]{1,0:T(8,128)(2,1)S(1)}, bf16[192,2048]{1,0:T(8,128)(2,1)}) custom-call(bf16[192,2048]{1,0:T(8,128)(2,1)S(1)} %bitcast.66, bf16[192,2048]{1,0:T(8,128)(2,1)} %bitcast.16.rows_grad, bf16[32,192,1408]{2,1,0:T(8,128)(2,1)} %bitcast.75), custom_call_target="tpu_custom_call" | custom-call | flops 6643777536 | bytes 20971520 | tf_op jit(solution)/shard_map/pallas_call | solution.py:192
  187.9 17.4 %all_to_all.21 = bf16[8,24,2048]{2,1,0:T(8,128)(2,1)S(1)} all-to-all(bf16[8,24,2048]{2,1,0:T(8,128)(2,1)S(1)} %bitcast.67), channel_id=1, replica_groups=mesh['seq'=32,'exp'=8] {'exp'}, dimensions={0} | all-to-all | bytes 1572864 | tf_op jit(solution)/shard_map/all_to_all | solution.py:261
  205.3 3.5 %all-to-all-start.3 = ((bf16[8,24,2048]{2,1,0:T(8,128)(2,1)}), bf16[8,24,2048]{2,1,0:T(8,128)(2,1)S(1)}, u32[]{:S(2)}, u32[]{:S(2)}) async-start(bf16[8,24,2048]{2,1,0:T(8,128)(2,1)} %bitcast.24), calls=%async_computation.3 | async-start | bytes 1572864 | tf_op jit(solution)/shard_map/all_to_all | solution.py:261
  208.9 13.0 %all-to-all-done.3 = bf16[8,24,2048]{2,1,0:T(8,128)(2,1)S(1)} async-done(((bf16[8,24,2048]{2,1,0:T(8,128)(2,1)}), bf16[8,24,2048]{2,1,0:T(8,128)(2,1)S(1)}, u32[]{:S(2)}, u32[]{:S(2)}) %all-to-all-start.3) | async-done | bytes 786464 | tf_op jit(solution)/shard_map/all_to_all | solution.py:261
  221.9 1.7 shard_map.143
  223.6 0.6 copy.67
  (44 shorter events, 1.5 us)
Async XLA Ops:
  7.2 77.7 %copy-start = (bf16[512,256]{1,0:T(8,128)(2,1)S(1)}, bf16[512,256]{1,0:T(8,128)(2,1)}, u32[]{:S(2)}) copy-start(bf16[512,256]{1,0:T(8,128)(2,1)} %param.13) | copy-start | bytes 786436
  7.2 2.2 copy-start.6
  7.2 5.6 %copy-start.5 = (bf16[512,256]{1,0:T(8,128)(2,1)S(1)}, bf16[512,256]{1,0:T(8,128)(2,1)}, u32[]{:S(2)}) copy-start(bf16[512,256]{1,0:T(8,128)(2,1)} %param.14) | copy-start | bytes 786436
  7.2 16.7 %copy-start.2 = (bf16[256,2048]{1,0:T(8,128)(2,1)S(1)}, bf16[256,2048]{1,0:T(8,128)(2,1)}, u32[]{:S(2)}) copy-start(bf16[256,2048]{1,0:T(8,128)(2,1)} %w_own.1) | copy-start | bytes 3145732
  7.2 161.8 %all-gather.3.cloned.1.call-start = ((), (), s32[]{:S(2)}) async-start(), calls=%async_computation.4 | async-start | bytes 17842176 | tf_op jit(solution)/shard_map/all_gather | solution.py:249
  9.4 11.1 %collective-permute-start = (bf16[512,256]{1,0:T(8,128)(2,1)S(1)}, bf16[512,256]{1,0:T(8,128)(2,1)S(1)}, u32[]{:S(2)}, u32[]{:S(2)}) collective-permute-start(bf16[512,256]{1,0:T(8,128)(2,1)S(1)} %copy-done.6), channel_id=1, source_target_pairs={{0,8},{8,16},{16,24},{24,32},{32,40},{40,48},{48,56},{56,64},{64,7... | collective-permute-start | bytes 786440 | tf_op jit(solution)/shard_map/ppermute | solution.py:40
  12.9 13.1 %collective-permute-start.4 = (bf16[512,256]{0,1:T(8,128)(2,1)S(1)}, bf16[512,256]{0,1:T(8,128)(2,1)S(1)}, u32[]{:S(2)}, u32[]{:S(2)}) collective-permute-start(bf16[512,256]{0,1:T(8,128)(2,1)S(1)} %copy.56), channel_id=1, source_target_pairs={{0,8},{8,16},{16,24},{24,32},{32,40},{40,48},{48,56},{56,64},{64,7... | collective-permute-start | bytes 786440 | tf_op jit(solution)/shard_map/ppermute | solution.py:40
  20.5 15.0 %collective-permute-start.1 = (bf16[512,256]{1,0:T(8,128)(2,1)S(1)}, bf16[512,256]{1,0:T(8,128)(2,1)}, u32[]{:S(2)}, u32[]{:S(2)}) collective-permute-start(bf16[512,256]{1,0:T(8,128)(2,1)S(1)} %collective-permute-done), channel_id=1, source_target_pairs={{0,8},{8,16},{16,24},{24,32},{32,40},{40,48},{48,56},{56,64},{64,7... | collective-permute-start | bytes 786440 | tf_op jit(solution)/shard_map/ppermute | solution.py:40
  23.9 89.5 %collective-permute-start.9 = (bf16[256,2048]{1,0:T(8,128)(2,1)S(1)}, bf16[256,2048]{1,0:T(8,128)(2,1)S(1)}, u32[]{:S(2)}, u32[]{:S(2)}) collective-permute-start(bf16[256,2048]{1,0:T(8,128)(2,1)S(1)} %copy-done.2), channel_id=1, source_target_pairs={{0,1},{1,0},{2,3},{3,2},{4,5},{5,4},{6,7},{7,6},{8,9},{9,8},{10,11... | collective-permute-start | bytes 3145736 | tf_op jit(solution)/shard_map/ppermute | solution.py:48
  26.1 18.0 %collective-permute-start.5 = (bf16[512,256]{0,1:T(8,128)(2,1)S(1)}, bf16[512,256]{0,1:T(8,128)(2,1)}, u32[]{:S(2)}, u32[]{:S(2)}) collective-permute-start(bf16[512,256]{0,1:T(8,128)(2,1)S(1)} %collective-permute-done.4), channel_id=1, source_target_pairs={{0,8},{8,16},{16,24},{24,32},{32,40},{40,48},{48,56},{56,64},{64,7... | collective-permute-start | bytes 786440 | tf_op jit(solution)/shard_map/ppermute | solution.py:40
  35.5 16.3 %collective-permute-start.2 = (bf16[512,256]{1,0:T(8,128)(2,1)}, bf16[512,256]{1,0:T(8,128)(2,1)}, u32[]{:S(2)}, u32[]{:S(2)}) collective-permute-start(bf16[512,256]{1,0:T(8,128)(2,1)} %collective-permute-done.1), channel_id=1, source_target_pairs={{0,8},{8,16},{16,24},{24,32},{32,40},{40,48},{48,56},{56,64},{64,7... | collective-permute-start | bytes 786440 | tf_op jit(solution)/shard_map/ppermute | solution.py:40
  44.1 14.1 %collective-permute-start.6 = (bf16[512,256]{0,1:T(8,128)(2,1)}, bf16[512,256]{0,1:T(8,128)(2,1)}, u32[]{:S(2)}, u32[]{:S(2)}) collective-permute-start(bf16[512,256]{0,1:T(8,128)(2,1)} %collective-permute-done.5), channel_id=1, source_target_pairs={{0,8},{8,16},{16,24},{24,32},{32,40},{40,48},{48,56},{56,64},{64,7... | collective-permute-start | bytes 786440 | tf_op jit(solution)/shard_map/ppermute | solution.py:40
  51.7 17.6 %collective-permute-start.3 = (bf16[512,256]{1,0:T(8,128)(2,1)}, bf16[512,256]{1,0:T(8,128)(2,1)}, u32[]{:S(2)}, u32[]{:S(2)}) collective-permute-start(bf16[512,256]{1,0:T(8,128)(2,1)} %collective-permute-done.2), channel_id=1, source_target_pairs={{0,8},{8,16},{16,24},{24,32},{32,40},{40,48},{48,56},{56,64},{64,7... | collective-permute-start | bytes 786440 | tf_op jit(solution)/shard_map/ppermute | solution.py:40
  58.1 20.0 %collective-permute-start.7 = (bf16[512,256]{0,1:T(8,128)(2,1)}, bf16[512,256]{0,1:T(8,128)(2,1)}, u32[]{:S(2)}, u32[]{:S(2)}) collective-permute-start(bf16[512,256]{0,1:T(8,128)(2,1)} %collective-permute-done.6), channel_id=1, source_target_pairs={{0,8},{8,16},{16,24},{24,32},{32,40},{40,48},{48,56},{56,64},{64,7... | collective-permute-start | bytes 786440 | tf_op jit(solution)/shard_map/ppermute | solution.py:40
  106.3 0.7 copy-start.7
  106.3 1.4 copy-start.1
  106.7 6.7 %collective-permute-start.8 = (bf16[4,64,256]{2,1,0:T(8,128)(2,1)S(1)}, bf16[4,64,256]{2,1,0:T(8,128)(2,1)S(1)}, u32[]{:S(2)}, u32[]{:S(2)}) collective-permute-start(bf16[4,64,256]{2,1,0:T(8,128)(2,1)S(1)} %get-tuple-element.27), channel_id=1, source_target_pairs={{0,1},{1,0},{2,3},{3,2},{4,5},{5,4},{6,7},{7,6},{8,9},{9,8},{10,11... | collective-permute-start | bytes 393224 | tf_op jit(solution)/shard_map/ppermute | solution.py:48
  108.9 29.5 %all-to-all-start.1 = ((bf16[8,24,2048]{2,1,0:T(8,128)(2,1)}), bf16[8,24,2048]{2,1,0:T(8,128)(2,1)}, u32[]{:S(2)}, u32[]{:S(2)}) async-start(bf16[8,24,2048]{2,1,0:T(8,128)(2,1)} %bitcast.15), calls=%async_computation.1 | async-start | bytes 1572864 | tf_op jit(solution)/shard_map/all_to_all | solution.py:261
  115.0 22.8 %copy-start.3 = (bf16[64,2048]{1,0:T(8,128)(2,1)S(1)}, bf16[64,2048]{1,0:T(8,128)(2,1)}, u32[]{:S(2)}) copy-start(bf16[64,2048]{1,0:T(8,128)(2,1)} %x.1) | copy-start | bytes 786436
  115.0 22.8 %copy-start.4 = (f32[2048]{0:T(1024)S(1)}, f32[2048]{0:T(1024)}, u32[]{:S(2)}) copy-start(f32[2048]{0:T(1024)} %param.17) | copy-start | bytes 24580
  115.1 16.9 %collective-permute-start.10 = (bf16[64,2048]{1,0:T(8,128)(2,1)S(1)}, bf16[64,2048]{1,0:T(8,128)(2,1)S(1)}, u32[]{:S(2)}, u32[]{:S(2)}) collective-permute-start(bf16[64,2048]{1,0:T(8,128)(2,1)S(1)} %get-tuple-element.25), channel_id=1, source_target_pairs={{0,2},{1,3},{2,4},{3,5},{4,6},{5,7},{6,0},{7,1},{8,10},{9,11},{10,... | collective-permute-start | bytes 786440 | tf_op jit(solution)/shard_map/ppermute | solution.py:44
  117.2 20.6 %collective-permute-start.11 = (bf16[64,2048]{1,0:T(8,128)(2,1)S(1)}, bf16[64,2048]{1,0:T(8,128)(2,1)S(1)}, u32[]{:S(2)}, u32[]{:S(2)}) collective-permute-start(bf16[64,2048]{1,0:T(8,128)(2,1)S(1)} %get-tuple-element.24), channel_id=1, source_target_pairs={{0,4},{1,5},{2,6},{3,7},{4,0},{5,1},{6,2},{7,3},{8,12},{9,13},{10,... | collective-permute-start | bytes 786440 | tf_op jit(solution)/shard_map/ppermute | solution.py:44
  119.9 18.0 %collective-permute-start.12 = (bf16[64,2048]{1,0:T(8,128)(2,1)S(1)}, bf16[64,2048]{1,0:T(8,128)(2,1)S(1)}, u32[]{:S(2)}, u32[]{:S(2)}) collective-permute-start(bf16[64,2048]{1,0:T(8,128)(2,1)S(1)} %get-tuple-element.23), channel_id=1, source_target_pairs={{0,6},{1,7},{2,0},{3,1},{4,2},{5,3},{6,4},{7,5},{8,14},{9,15},{10,... | collective-permute-start | bytes 786440 | tf_op jit(solution)/shard_map/ppermute | solution.py:44
  187.9 20.9 %copy-start.8 = (f32[64,2]{0,1:T(2,128)S(1)}, f32[64,2]{0,1:T(2,128)}, u32[]{:S(2)}) copy-start(f32[64,2]{0,1:T(2,128)} %param.22) | copy-start | bytes 1540
  205.3 16.6 %all-to-all-start.3 = ((bf16[8,24,2048]{2,1,0:T(8,128)(2,1)}), bf16[8,24,2048]{2,1,0:T(8,128)(2,1)S(1)}, u32[]{:S(2)}, u32[]{:S(2)}) async-start(bf16[8,24,2048]{2,1,0:T(8,128)(2,1)} %bitcast.24), calls=%async_computation.3 | async-start | bytes 1572864 | tf_op jit(solution)/shard_map/all_to_all | solution.py:261
Sparse Core Ops, SparseCore 0:
  10.6 158.3 all-gather.2
